TPU v7x, 512 devices: a whole 4x4x16 slice. The times are simulated.
512 devices in a mesh: dp: 32 (over x, y, core), expert: 16 (over z).
Axes of the slice: x: 4, y: 4, z: 16, core: 2. Of those that a mesh axis runs over, the one named last changes fastest.
Arguments:
- grad_out: bfloat16 [2048, 6144], P('expert', 'dp'), may hold values from -48 to 48
- routes: int32 [2048, 4], P('expert'), may hold values from 0 to 15, all different within a row; in each aligned block of 128 rows (0 to 127, 128 to 255, ...) at most 40 rows name the same one
- probs: float32 [2048, 4], P('expert'), may hold values from 0.05 to 0.6
- resp_len: int32 [16, 4], P('expert'), may hold values from 1 to 64, 128 in all within a row
- w_down: bfloat16 [16, 5376, 6144], P('expert', 'dp'), may hold values from -0.078125 to 0.078125
- w_up: bfloat16 [16, 6144, 5376], P('expert', 'dp'), may hold values from -0.078125 to 0.078125
- gate_act: bfloat16 [16, 640, 5376], P('expert', None, 'dp'), may hold values from -6 to 6
Outputs:
- grad_in: bfloat16 [2048, 6144], P('expert', 'dp')
Inputs may be any that keep to these rules, and one draw needn't show every extreme that they name: `routes`: within each aligned block of 128 rows (one shard) no expert is named more than 40 times, a bound that some block reaches. `resp_len`: each row sums to 128, and its largest entry is 64.
All inputs are finite; a program needn't handle non-finite values.
Results may differ from a plain program's by a relative error of at most 0.013.
Values may be sent and summed in bfloat16 or wider, within the bound.
No kernel may reach another device: no remote copies, remote signals or barrier semaphores. Data moves between devices by JAX's collectives and lax.ppermute only.
A program may use at most 64 MiB of HBM per device.

v0:
```python
import jax
import jax.numpy as jnp
from jax import lax
from jax.sharding import PartitionSpec as P


def token_weight(resp_len, rows):
    lengths = resp_len[0]
    ends = jnp.cumsum(lengths)
    starts = ends - lengths
    position = jnp.arange(rows, dtype=jnp.int32)[:, None]
    inside = (position >= starts[None, :]) & (position < ends[None, :])
    inverse = 1.0 / lengths.astype(jnp.float32)
    return jnp.sum(jnp.where(inside, inverse[None, :], jnp.zeros_like(inverse)[None, :]), axis=1)


def slot_index(routes, experts, capacity):
    labels = jnp.arange(experts, dtype=jnp.int32)
    hits = (routes[:, :, None] == labels[None, None, :]).astype(jnp.int32)
    per_row = jnp.sum(hits, axis=1)
    before = jnp.cumsum(per_row, axis=0) - per_row
    position = jnp.sum(hits * before[:, None, :], axis=2)
    return routes * capacity + position


def contract(left, right):
    return lax.dot_general(
        left, right, (((1,), (1,)), ((), ())), preferred_element_type=jnp.float32
    )


def on_device(grad_out, routes, probs, resp_len, w_down, w_up, gate_act):
    tokens_here, width_here = grad_out.shape
    picks = routes.shape[1]
    experts = lax.axis_size("expert")
    capacity = min(
        tokens_here, tokens_here * picks // experts + tokens_here * picks // (4 * experts)
    )
    slots = experts * capacity
    weight = token_weight(resp_len, tokens_here)
    target = slot_index(routes, experts, capacity).reshape(-1)
    factor = probs * weight[:, None]
    scaled = (grad_out[:, None, :].astype(jnp.float32) * factor[:, :, None]).astype(jnp.bfloat16)
    selector = (jnp.arange(slots, dtype=jnp.int32)[:, None] == target[None, :]).astype(jnp.bfloat16)
    outgoing = jnp.dot(
        selector,
        scaled.reshape(tokens_here * picks, width_here),
        preferred_element_type=jnp.float32,
    ).astype(jnp.bfloat16)
    arrived = lax.all_to_all(
        outgoing.reshape(experts, capacity, width_here),
        "expert",
        split_axis=0,
        concat_axis=0,
        tiled=True,
    ).reshape(slots, width_here)
    down_rows = w_down[0]
    up_rows = w_up[0]
    saved = gate_act[0]
    full_rows = lax.all_gather(arrived, "dp", axis=1, tiled=True)
    hidden_sum = contract(full_rows, down_rows)
    hidden_grad = (hidden_sum * saved.astype(jnp.float32)).astype(jnp.bfloat16)
    full_hidden = lax.all_gather(hidden_grad, "dp", axis=1, tiled=True)
    product = contract(full_hidden, up_rows)
    returning = product.astype(jnp.bfloat16)
    back = lax.all_to_all(
        returning.reshape(experts, capacity, width_here),
        "expert",
        split_axis=0,
        concat_axis=0,
        tiled=True,
    ).reshape(slots, width_here)
    picked = (
        jnp.take(back, target, axis=0).reshape(tokens_here, picks, width_here).astype(jnp.float32)
    )
    return jnp.sum(picked, axis=1).astype(jnp.bfloat16)


def solution(mesh):
    in_specs = (
        P("expert", "dp"),
        P("expert", None),
        P("expert", None),
        P("expert", None),
        P("expert", "dp", None),
        P("expert", "dp", None),
        P("expert", None, "dp"),
    )
    out_specs = P("expert", "dp")
    return jax.shard_map(
        on_device, mesh=mesh, in_specs=in_specs, out_specs=out_specs, check_vma=False
    )
```

profile of v0, /device:TPU:2, one launch (start us, length us, event | category | flops | bytes accessed | tf_op | source)
XLA Modules:
  0.0 234.0 jit_solution(2945897742113075317)
XLA Ops:
  6.5 0.8 divide_bitcast_fusion
  7.3 0.8 reduce-window.4
  8.2 0.7 fusion.18
  8.8 0.7 convert_reduce_fusion
  9.5 0.1 copy.30
  9.7 0.7 broadcast_multiply_fusion
  10.4 0.1 copy.36
  10.5 0.1 mul.51
  10.6 0.2 reduce_window_sum.18
  10.9 0.7 select_reduce_fusion.1
  11.6 0.7 compare_and_fusion
  12.3 0.1 copy.34
  12.4 0.1 reshape.88
  12.5 0.9 copy.35
  13.4 0.1 mul.47
  13.5 0.2 mul.48
  13.7 0.5 fusion.8
  14.2 0.2 copy.37
  14.4 35.8 %all_to_all.10 = bf16[16,40,192]{2,1,0:T(8,128)(2,1)S(1)} all-to-all(bf16[16,40,192]{2,1,0:T(8,128)(2,1)S(1)} %bitcast.33), channel_id=1, replica_groups=mesh['dp'=32,'expert'=16] {'expert'}, dimensions={0} | all-to-all | bytes 491520 | tf_op jit(solution)/shard_map/all_to_all | solution.py:50
  50.2 0.9 copy.38
  51.1 62.5 %all-gather.3.cloned.1.call-done = bf16[640,6144]{0,1:T(8,128)(2,1)} async-done(((bf16[640,192]{0,1:T(8,128)(2,1)}), bf16[640,6144]{0,1:T(8,128)(2,1)}) %all-gather.3.cloned.1.call-update) | async-done | bytes 7864336 | tf_op jit(solution)/shard_map/all_gather | solution.py:60
  113.6 6.3 %fusion.12 = bf16[640,168]{0,1:T(8,128)(2,1)} fusion(bf16[640,6144]{0,1:T(8,128)(2,1)} %all-gather.3.cloned.1.call-done, bf16[1,168,6144]{2,1,0:T(8,128)(2,1)} %param.11, bf16[1,640,168]{1,2,0:T(8,128)(2,1)} %param.13), kind=kOutput, calls=%fused_computation.10 | convolution fusion | flops 1321528320 | bytes 10358784 | tf_op jit(solution)/shard_map/dot_general | solution.py:27
  120.0 64.6 %all-gather.5.cloned.1.call-done = bf16[640,5376]{0,1:T(8,128)(2,1)} async-done(((bf16[640,168]{0,1:T(8,128)(2,1)}), bf16[640,5376]{0,1:T(8,128)(2,1)}) %all-gather.5.cloned.1.call-update) | async-done | bytes 6881296 | tf_op jit(solution)/shard_map/all_gather | solution.py:63
  184.6 4.7 %fusion.9 = bf16[640,192]{0,1:T(8,128)(2,1)S(1)} fusion(bf16[640,5376]{0,1:T(8,128)(2,1)} %all-gather.5.cloned.1.call-done, bf16[1,192,5376]{2,1,0:T(8,128)(2,1)S(1)} %copy-done), kind=kOutput, calls=%fused_computation.9 | convolution fusion | flops 1321328640 | bytes 9191424 | tf_op jit(solution)/shard_map/dot_general | solution.py:27
  189.3 0.9 copy.39
  190.2 12.3 %all-to-all-start.1 = ((bf16[16,40,192]{2,1,0:T(8,128)(2,1)}), bf16[16,40,192]{2,1,0:T(8,128)(2,1)S(1)}, u32[]{:S(2)}, u32[]{:S(2)}) async-start(bf16[16,40,192]{2,1,0:T(8,128)(2,1)} %bitcast.10), calls=%async_computation.1 | async-start | bytes 655360 | tf_op jit(solution)/shard_map/all_to_all | solution.py:66
  202.5 0.1 reshape.95
  202.6 0.1 copy.33
  202.8 21.2 %all-to-all-done.1 = bf16[16,40,192]{2,1,0:T(8,128)(2,1)S(1)} async-done(((bf16[16,40,192]{2,1,0:T(8,128)(2,1)}), bf16[16,40,192]{2,1,0:T(8,128)(2,1)S(1)}, u32[]{:S(2)}, u32[]{:S(2)}) %all-to-all-start.1) | async-done | bytes 245792 | tf_op jit(solution)/shard_map/all_to_all | solution.py:66
  224.0 1.9 gather_fusion
  226.1 0.4 select_reduce_fusion
  226.4 0.7 copy.41
  (12 shorter events, 0.3 us)
Async XLA Ops:
  6.5 178.1 %copy-start = (bf16[1,192,5376]{2,1,0:T(8,128)(2,1)S(1)}, bf16[1,192,5376]{2,1,0:T(8,128)(2,1)}, u32[]{:S(2)}) copy-start(bf16[1,192,5376]{2,1,0:T(8,128)(2,1)} %param.12) | copy-start | bytes 6193156
  6.5 107.1 %all-gather.3.cloned.1.call-start = ((), (), s32[]{:S(2)}) async-start(), calls=%async_computation.2 | async-start | bytes 8110080 | tf_op jit(solution)/shard_map/all_gather | solution.py:60
  51.0 133.6 %all-gather.5.cloned.1.call-start = ((), (), s32[]{:S(2)}) async-start(), calls=%async_computation.3 | async-start | bytes 7096320 | tf_op jit(solution)/shard_map/all_gather | solution.py:63
  190.2 33.8 %all-to-all-start.1 = ((bf16[16,40,192]{2,1,0:T(8,128)(2,1)}), bf16[16,40,192]{2,1,0:T(8,128)(2,1)S(1)}, u32[]{:S(2)}, u32[]{:S(2)}) async-start(bf16[16,40,192]{2,1,0:T(8,128)(2,1)} %bitcast.10), calls=%async_computation.1 | async-start | bytes 655360 | tf_op jit(solution)/shard_map/all_to_all | solution.py:66
Sparse Core Ops, SparseCore 0:
  51.2 62.4 all-gather.2
  120.1 64.4 all-gather.4
where the time goes:
time: 234 us
  waiting for transfers between devices  148 us (63%)
  blocking collectives  35.8 us (15%)
  between operations  13.5 us (6%)
  starting transfers between devices  12.3 us (5%)
  matrix products  11.5 us (5%)
  local copies, waits for them, and re-layouts  6.7 us (3%)
  other arithmetic  5.74 us (2%)
    all_gather x1, waiting for transfers between devices, on_device(): full_hidden = lax.all_gather(hidden_grad, 'dp', axis=1, tiled=True)  64.6 us
    all_gather x1, waiting for transfers between devices, on_device(): full_rows = lax.all_gather(arrived, 'dp', axis=1, tiled=True)  62.5 us
    all_to_all x1, blocking collectives, on_device(): lax.all_to_all(outgoing.reshape(experts, capacity, width_here), 'expert',...  35.8 us
    all_to_all x1, waiting for transfers between devices, on_device(): lax.all_to_all(returning.reshape(experts, capacity, width_here), 'expert'...  21.2 us
    all_to_all x1, starting transfers between devices, on_device(): lax.all_to_all(returning.reshape(experts, capacity, width_here), 'expert'...  12.3 us
    dot_general x2, matrix products, contract(): lax.dot_general(left, right, (((1,), (1,)), ((), ())), preferred_element_...  11 us
  transfers between devices with their start and end apart: 3, of which 3 were waited for; matrix products, arithmetic and copies ran while one was open for 0% of the time, Pallas kernels for 0%

commit v1 on v0

--- a/solution.py
+++ b/solution.py
@@ -57,7 +57,8 @@
     down_rows = w_down[0]
     up_rows = w_up[0]
     saved = gate_act[0]
-    full_rows = lax.all_gather(arrived, "dp", axis=1, tiled=True)
+    repeated = jnp.stack([arrived] * lax.axis_size("dp"))
+    full_rows = jnp.concatenate(lax.all_to_all(repeated, "dp", 0, 0), axis=1)
     hidden_sum = contract(full_rows, down_rows)
     hidden_grad = (hidden_sum * saved.astype(jnp.float32)).astype(jnp.bfloat16)
     full_hidden = lax.all_gather(hidden_grad, "dp", axis=1, tiled=True)

time: 234 us -> 258 us (1.10)
  blocking collectives: 35.8 us -> 132 us
  waiting for transfers between devices: 148 us -> 79.5 us
  matrix products: 11.5 us -> 7.83 us
    all_to_all x0 -> x1, blocking collectives: none -> 95.9 us  [on_device(): full_rows = jnp.concatenate(lax.all_to_all(repeated, 'dp', 0, 0), axis=1)]
    all_gather x1 -> x0, waiting for transfers between devices: 62.5 us -> none  [on_device(): full_rows = lax.all_gather(arrived, 'dp', axis=1, tiled=True)]
    all_gather x1, waiting for transfers between devices: 64.6 us -> 58.3 us  [on_device(): full_hidden = lax.all_gather(hidden_grad, 'dp', axis=1, tiled=True)]
    dot_general x2, matrix products: 11 us -> 7.33 us  [contract(): lax.dot_general(left, right, (((1,), (1,)), ((), ())), preferred_element_...]
  transfers between devices with their start and end apart: 3 -> 2, of which waited for: 3 -> 2; matrix products, arithmetic and copies ran while one was open for 0% -> 0% of each run, Pallas kernels for 0% -> 0%
where the time goes in v1:
time: 258 us
  blocking collectives  132 us (51%)
  waiting for transfers between devices  79.5 us (31%)
  between operations  13.5 us (5%)
  starting transfers between devices  12.3 us (5%)
  matrix products  7.83 us (3%)
  local copies, waits for them, and re-layouts  7.09 us (3%)
  other arithmetic  5.74 us (2%)
    all_to_all x1, blocking collectives, on_device(): full_rows = jnp.concatenate(lax.all_to_all(repeated, 'dp', 0, 0), axis=1)  95.9 us
    all_gather x1, waiting for transfers between devices, on_device(): full_hidden = lax.all_gather(hidden_grad, 'dp', axis=1, tiled=True)  58.3 us
    all_to_all x1, blocking collectives, on_device(): lax.all_to_all(outgoing.reshape(experts, capacity, width_here), 'expert',...  35.8 us
    all_to_all x1, waiting for transfers between devices, on_device(): lax.all_to_all(returning.reshape(experts, capacity, width_here), 'expert'...  21.2 us
    all_to_all x1, starting transfers between devices, on_device(): lax.all_to_all(returning.reshape(experts, capacity, width_here), 'expert'...  12.3 us
    dot_general x2, matrix products, contract(): lax.dot_general(left, right, (((1,), (1,)), ((), ())), preferred_element_...  7.33 us
  transfers between devices with their start and end apart: 2, of which 2 were waited for; matrix products, arithmetic and copies ran while one was open for 0% of the time, Pallas kernels for 0%

profile of v1, /device:TPU:2, one launch (start us, length us, event | category | flops | bytes accessed | tf_op | source)
XLA Modules:
  0.0 257.6 jit_solution(14835909791957190649)
XLA Ops:
  6.5 0.8 divide_bitcast_fusion
  7.3 0.8 reduce-window.4
  8.2 0.7 fusion.18
  8.8 0.7 convert_reduce_fusion
  9.5 0.1 copy.32
  9.7 0.7 broadcast_multiply_fusion
  10.4 0.1 copy.38
  10.5 0.1 mul.51
  10.6 0.2 reduce_window_sum.18
  10.9 0.7 select_reduce_fusion.1
  11.6 0.7 compare_and_fusion
  12.3 0.1 copy.36
  12.4 0.1 reshape.93
  12.5 0.9 copy.37
  13.5 0.2 mul.48
  13.7 0.5 fusion.8
  14.2 0.2 copy.39
  14.4 35.8 %all_to_all.15 = bf16[16,40,192]{2,1,0:T(8,128)(2,1)S(1)} all-to-all(bf16[16,40,192]{2,1,0:T(8,128)(2,1)S(1)} %bitcast.37), channel_id=1, replica_groups=mesh['dp'=32,'expert'=16] {'expert'}, dimensions={0} | all-to-all | bytes 491520 | tf_op jit(solution)/shard_map/all_to_all | solution.py:50
  50.2 0.2 copy.40
  50.3 1.1 stack.3
  51.4 95.9 %all_to_all.16 = bf16[32,640,192]{1,2,0:T(8,128)(2,1)S(1)} all-to-all(bf16[32,640,192]{1,2,0:T(8,128)(2,1)S(1)} %stack.3), channel_id=1, replica_groups=mesh['dp'=32,'expert'=16] {'dp'}, dimensions={0} | all-to-all | bytes 15728640 | tf_op jit(solution)/shard_map/all_to_all | solution.py:61
  147.3 2.6 %fusion.12 = bf16[640,168]{0,1:T(8,128)(2,1)} fusion(bf16[640,6144]{0,1:T(8,128)(2,1)S(1)} %bitcast.36, bf16[1,168,6144]{2,1,0:T(8,128)(2,1)S(1)} %copy-done.1, bf16[1,640,168]{1,2,0:T(8,128)(2,1)S(1)} %copy-done.2), kind=kOutput, calls=%fused_computation.10 | convolution fusion | flops 1321528320 | bytes 10358784 | tf_op jit(solution)/shard_map/dot_general | solution.py:27
  149.9 58.3 %all-gather.2.cloned.1.call-done = bf16[640,5376]{0,1:T(8,128)(2,1)} async-done(((bf16[640,168]{0,1:T(8,128)(2,1)}), bf16[640,5376]{0,1:T(8,128)(2,1)}) %all-gather.2.cloned.1.call-update) | async-done | bytes 6881296 | tf_op jit(solution)/shard_map/all_gather | solution.py:64
  208.2 4.7 %fusion.9 = bf16[640,192]{0,1:T(8,128)(2,1)S(1)} fusion(bf16[640,5376]{0,1:T(8,128)(2,1)} %all-gather.2.cloned.1.call-done, bf16[1,192,5376]{2,1,0:T(8,128)(2,1)S(1)} %copy-done), kind=kOutput, calls=%fused_computation.9 | convolution fusion | flops 1321328640 | bytes 9191424 | tf_op jit(solution)/shard_map/dot_general | solution.py:27
  213.0 0.9 copy.41
  213.9 12.3 %all-to-all-start.2 = ((bf16[16,40,192]{2,1,0:T(8,128)(2,1)}), bf16[16,40,192]{2,1,0:T(8,128)(2,1)S(1)}, u32[]{:S(2)}, u32[]{:S(2)}) async-start(bf16[16,40,192]{2,1,0:T(8,128)(2,1)} %bitcast.12), calls=%async_computation.2 | async-start | bytes 655360 | tf_op jit(solution)/shard_map/all_to_all | solution.py:67
  226.1 0.1 reshape.101
  226.3 0.1 copy.35
  226.4 21.2 %all-to-all-done.2 = bf16[16,40,192]{2,1,0:T(8,128)(2,1)S(1)} async-done(((bf16[16,40,192]{2,1,0:T(8,128)(2,1)}), bf16[16,40,192]{2,1,0:T(8,128)(2,1)S(1)}, u32[]{:S(2)}, u32[]{:S(2)}) %all-to-all-start.2) | async-done | bytes 245792 | tf_op jit(solution)/shard_map/all_to_all | solution.py:67
  247.6 1.9 gather_fusion
  249.7 0.4 select_reduce_fusion
  250.1 0.7 copy.43
  (15 shorter events, 0.4 us)
Async XLA Ops:
  6.5 201.7 %copy-start = (bf16[1,192,5376]{2,1,0:T(8,128)(2,1)S(1)}, bf16[1,192,5376]{2,1,0:T(8,128)(2,1)}, u32[]{:S(2)}) copy-start(bf16[1,192,5376]{2,1,0:T(8,128)(2,1)} %param.12) | copy-start | bytes 6193156
  6.5 201.7 %all-gather.2.cloned.1.call-start = ((), (), s32[]{:S(2)}) async-start(), calls=%async_computation.3 | async-start | bytes 7096320 | tf_op jit(solution)/shard_map/all_gather | solution.py:64
  51.4 95.9 %copy-start.1 = (bf16[1,168,6144]{2,1,0:T(8,128)(2,1)S(1)}, bf16[1,168,6144]{2,1,0:T(8,128)(2,1)}, u32[]{:S(2)}) copy-start(bf16[1,168,6144]{2,1,0:T(8,128)(2,1)} %param.11) | copy-start | bytes 6193156
  51.4 95.9 %copy-start.2 = (bf16[1,640,168]{1,2,0:T(8,128)(2,1)S(1)}, bf16[1,640,168]{1,2,0:T(8,128)(2,1)}, u32[]{:S(2)}) copy-start(bf16[1,640,168]{1,2,0:T(8,128)(2,1)} %param.13) | copy-start | bytes 645124
  213.9 33.8 %all-to-all-start.2 = ((bf16[16,40,192]{2,1,0:T(8,128)(2,1)}), bf16[16,40,192]{2,1,0:T(8,128)(2,1)S(1)}, u32[]{:S(2)}, u32[]{:S(2)}) async-start(bf16[16,40,192]{2,1,0:T(8,128)(2,1)} %bitcast.12), calls=%async_computation.2 | async-start | bytes 655360 | tf_op jit(solution)/shard_map/all_to_all | solution.py:67
Sparse Core Ops, SparseCore 0:
  150.1 58.1 all-gather.1
